TPU v7x, 128 devices: a whole 4x4x4 slice. The times are simulated.
128 devices in a mesh: dp: 32 (over x, y, z_hi), narrow: 4 (over z_lo, core).
Axes of the slice: x: 4, y: 4, z: 4 (z_hi: 2, z_lo: 2; z = z_hi * 2 + z_lo), core: 2. Of those that a mesh axis runs over, the one named last changes fastest.
Arguments:
- picture_features: bfloat16 [98304, 1152], P(('dp', 'narrow')), may hold values from -1.0234375 to 1.0234375
- caption_features: bfloat16 [98304, 1152], P(('dp', 'narrow')), may hold values from -1.0234375 to 1.0234375
- match_identifiers: int32 [98304], replicated, may hold values from 0 to 767
- trading_step_number: int32 [1], replicated, may hold values from 1 to 31
- sharpness_coefficient: float32 [1], replicated, may hold values from 0.5 to 2
- offset_term: float32 [1], replicated, may hold values from -2 to 0
Outputs:
- grad_image: float32 [98304, 1152], P(('dp', 'narrow'))
- text_embedding_gradient: float32 [98304, 1152], P(('dp', 'narrow'))
- row_loss: float32 [98304], P(('dp', 'narrow'))
All inputs are finite; a program needn't handle non-finite values.
Results may differ from a plain program's by a relative error of at most 0.0034.
Values may be sent and summed in bfloat16 or wider, within the bound.
No kernel may reach another device: no remote copies, remote signals or barrier semaphores. Data moves between devices by JAX's collectives and lax.ppermute only.
A program may use at most 128 MiB of HBM per device.

v0:
```python
import jax
import jax.numpy as jnp
from jax import lax
from jax.sharding import PartitionSpec as P

AXES = ("dp", "narrow")


def xor_route(count, mask):
    return [(d, d ^ mask) for d in range(count)]


def pair_terms(logits, left_ids, right_ids):
    same = left_ids[:, None] == right_ids[None, :]
    z = jnp.where(same, logits, -logits)
    tail = jnp.exp(-jnp.abs(z))
    pair_loss = jnp.maximum(-z, 0.0) + jnp.log1p(tail)
    share = jnp.where(z > 0, tail, 1.0) / (1.0 + tail)
    coef = jnp.where(same, -share, share).astype(jnp.bfloat16)
    return pair_loss, coef


def dot(a, b, dims):
    return lax.dot_general(a, b, (dims, ((), ())), preferred_element_type=jnp.float32)


def partner_mask(rnd, width):
    return rnd * width ^ (rnd & 1) * (width // 2)


def solution(mesh):
    groups, width = mesh.shape["dp"], mesh.shape["narrow"]
    count, half = groups * width, width // 2
    over_z = xor_route(count, half)
    over_core = xor_route(count, 1)

    def over_dp(rnd, block):
        return lax.ppermute(block, AXES, xor_route(count, partner_mask(rnd, width)))

    def by_round(step, which, *args):
        branches = [lambda *a, r=r: step(r, *a) for r in range(1, groups)]
        return lax.switch(which, branches, *args)

    def per_device(picture, caption, ids, rnd, scale, shift):
        rnd, scale, shift = rnd[0], scale[0], shift[0]
        rows = picture.shape[0]
        me = lax.axis_index("dp") * width + lax.axis_index("narrow")
        text_at = me ^ partner_mask(rnd, width)
        take = lambda device: lax.dynamic_slice_in_dim(ids, device * rows, rows)
        image_ids = jnp.concatenate([take(me), take(me ^ half)])
        text_ids = jnp.concatenate([take(text_at), take(text_at ^ 1)])

        image_far = lax.ppermute(picture, AXES, over_z)
        text_own = by_round(over_dp, rnd - 1, caption)
        text_near = lax.ppermute(text_own, AXES, over_core)
        images = jnp.concatenate([picture, image_far])
        texts = jnp.concatenate([text_own, text_near])

        logits = scale * dot(images, texts, ((1,), (1,))) + shift
        pair_loss, coef = pair_terms(logits, image_ids, text_ids)
        loss_sum = jnp.sum(pair_loss, axis=1)

        text_parts = lax.optimization_barrier(scale * dot(coef, images, ((0,), (0,))))
        text_far_part = lax.ppermute(text_parts[rows:], AXES, over_core)
        image_far_part = (scale * dot(coef[rows:], texts, ((1,), (0,)))).astype(jnp.bfloat16)
        text_part = (text_parts[:rows] + text_far_part).astype(jnp.bfloat16)

        loss_far = lax.ppermute(loss_sum[rows:], AXES, over_z)
        image_far_part, loss_far = lax.optimization_barrier((image_far_part, loss_far))
        image_far_part = lax.ppermute(image_far_part, AXES, over_z)
        text_grad = by_round(over_dp, rnd - 1, text_part)
        text_grad, image_far_part = lax.optimization_barrier((text_grad, image_far_part))
        image_grad = scale * dot(coef[:rows], texts, ((1,), (0,))) + image_far_part.astype(jnp.float32)
        row_loss = (loss_sum[:rows] + loss_far) / (rows * width)
        return image_grad, text_grad.astype(jnp.float32), row_loss

    in_specs = (P(AXES, None), P(AXES, None), P(), P(), P(), P())
    out_specs = (P(AXES, None), P(AXES, None), P(AXES))
    return jax.shard_map(
        per_device, mesh=mesh, in_specs=in_specs, out_specs=out_specs, check_vma=False
    )
```

profile of v0, /device:TPU:0, one launch (start us, length us, event | category | flops | bytes accessed | tf_op | source)
XLA Modules:
  0.0 137.5 jit_solution(6784689476723536490)
XLA Ops:
  0.6 2.1 %collective-permute-start.62 = (bf16[768,1152]{1,0:T(8,128)(2,1)}, bf16[768,1152]{1,0:T(8,128)(2,1)S(1)}, u32[]{:S(2)}, u32[]{:S(2)}) collective-permute-start(bf16[768,1152]{1,0:T(8,128)(2,1)} %param.68), channel_id=1, source_target_pairs={{0,2},{1,3},{2,0},{3,1},{4,6},{5,7},{6,4},{7,5},{8,10},{9,11},{10,... | collective-permute-start | bytes 5308424 | tf_op jit(solution)/shard_map/ppermute | solution.py:53
  3.4 44.1 %conditional.2 = (bf16[768,1152]{1,0:T(8,128)(2,1)}) conditional(s32[]{:T(128)} %bitcast.2, bf16[768,1152]{1,0:T(8,128)(2,1)} %param.69, bf16[768,1152]{1,0:T(8,128)(2,1)} %param.69, bf16[768,1152]{1,0:T(8,128)(2,1)} %param.69, bf16[768,1152]{1,0:T(8,128)(2,1)} %param.69, bf16[768,1152]{1,0:T(8,128)(2,1)} %param.69, ...), branch_computations={%region_0.0_spmd, %region_1.0_spmd, %region_2.0_spmd, %region_3.0_... | conditional | bytes 7077936 | solution.py:42
  3.4 5.1 %collective-permute-start.16 = (bf16[768,1152]{1,0:T(8,128)(2,1)}, bf16[768,1152]{1,0:T(8,128)(2,1)}, u32[]{:S(2)}, u32[]{:S(2)}) collective-permute-start(bf16[768,1152]{1,0:T(8,128)(2,1)} %param.16), channel_id=1, source_target_pairs={{0,70},{1,71},{2,68},{3,69},{4,66},{5,67},{6,64},{7,65},{8,78},{9,... | collective-permute-start | bytes 5308424 | tf_op jit(solution)/shard_map/cond/branch_16_fun/ppermute | solution.py:38
  8.5 39.0 %collective-permute-done.16 = bf16[768,1152]{1,0:T(8,128)(2,1)} collective-permute-done((bf16[768,1152]{1,0:T(8,128)(2,1)}, bf16[768,1152]{1,0:T(8,128)(2,1)}, u32[]{:S(2)}, u32[]{:S(2)}) %collective-permute-start.16) | collective-permute-done | bytes 1769504 | tf_op jit(solution)/shard_map/cond/branch_16_fun/ppermute | solution.py:38
  47.5 0.0 collective-permute-start.63
  48.8 0.9 fusion.10
  49.7 1.6 %constant_dynamic-update-slice_fusion.1 = bf16[1536,1152]{1,0:T(8,128)(2,1)S(1)} fusion(bf16[768,1152]{1,0:T(8,128)(2,1)} %param.68), kind=kLoop, calls=%fused_computation.19 | loop fusion | bytes 3538944
  51.3 0.0 collective-permute-done.62
  51.3 0.3 constant_dynamic-update-slice_fusion
  51.6 0.0 collective-permute-done.63
  51.6 15.5 %add_reduce_fusion = (f32[1536]{0:T(1024)S(1)}, bf16[1536,1536]{0,1:T(8,128)(2,1)S(1)}) fusion(s32[1536]{0:T(1024)S(1)} %get-tuple-element.144, s32[1536]{0:T(1024)S(1)} %get-tuple-element.143, f32[]{:T(128)} %bitcast.11, bf16[1536,1152]{1,0:T(8,128)(2,1)S(1)} %constant_dynamic-update-slice_fusion, bf16[768,1152]{1,0:T(8,128)(2,1)S(1)} %collective-permute-done.63, ...), kind=kOutput, calls=%fused_computation.5 | convolution fusion | flops 5485361664 | bytes 11814920 | tf_op jit(solution)/shard_map/dot_general | solution.py:24
  67.1 6.3 %convolution_multiply_fusion = f32[1536,1152]{1,0:T(8,128)S(1)} fusion(bf16[1536,1536]{0,1:T(8,128)(2,1)S(1)} %get-tuple-element.138, bf16[1536,1152]{1,0:T(8,128)(2,1)S(1)} %constant_dynamic-update-slice_fusion, f32[]{:T(128)} %bitcast.9), kind=kOutput, calls=%fused_computation.2 | convolution fusion | flops 5437587456 | bytes 15335428 | tf_op jit(solution)/shard_map/dot_general | solution.py:24
  73.4 0.2 slice.26
  73.6 0.6 collective-permute-start.64
  74.2 0.6 collective-permute-start.65
  74.9 5.9 %fusion.3 = bf16[768,1152]{1,0:T(8,128)(2,1)} fusion(bf16[1536,1536]{0,1:T(8,128)(2,1)S(1)} %get-tuple-element.138, f32[]{:T(128)} %bitcast.10, bf16[768,1152]{1,0:T(8,128)(2,1)S(1)} %collective-permute-done.63, bf16[768,1152]{1,0:T(8,128)(2,1)} %get-tuple-element.145), kind=kOutput, calls=%fused_computation.13 | convolution fusion | flops 2726756352 | bytes 7667716 | tf_op jit(solution)/shard_map/dot_general | solution.py:24
  80.8 1.4 %collective-permute-start.66 = (bf16[768,1152]{1,0:T(8,128)(2,1)}, bf16[768,1152]{1,0:T(8,128)(2,1)}, u32[]{:S(2)}, u32[]{:S(2)}) collective-permute-start(bf16[768,1152]{1,0:T(8,128)(2,1)} %fusion.3), channel_id=1, source_target_pairs={{0,2},{1,3},{2,0},{3,1},{4,6},{5,7},{6,4},{7,5},{8,10},{9,11},{10,... | collective-permute-start | bytes 5308424 | tf_op jit(solution)/shard_map/ppermute | solution.py:70
  82.2 0.6 fusion.6
  82.8 0.5 fusion.2
  83.2 44.1 %conditional.3 = (bf16[768,1152]{1,0:T(8,128)(2,1)}) conditional(s32[]{:T(128)} %bitcast.2, bf16[768,1152]{1,0:T(8,128)(2,1)S(1)} %fusion.2, bf16[768,1152]{1,0:T(8,128)(2,1)S(1)} %fusion.2, bf16[768,1152]{1,0:T(8,128)(2,1)S(1)} %fusion.2, bf16[768,1152]{1,0:T(8,128)(2,1)S(1)} %fusion.2, ...), branch_computations={%region_31.32_spmd, %region_32.33_spmd, %region_33.34_spmd, %regio... | conditional | bytes 7077936 | solution.py:42
  83.3 5.1 %collective-permute-start.47 = (bf16[768,1152]{1,0:T(8,128)(2,1)S(1)}, bf16[768,1152]{1,0:T(8,128)(2,1)}, u32[]{:S(2)}, u32[]{:S(2)}) collective-permute-start(bf16[768,1152]{1,0:T(8,128)(2,1)S(1)} %param.47), channel_id=1, source_target_pairs={{0,70},{1,71},{2,68},{3,69},{4,66},{5,67},{6,64},{7,65},{8,78},{9,... | collective-permute-start | bytes 5308424 | tf_op jit(solution)/shard_map/cond/branch_16_fun/ppermute | solution.py:38
  88.3 39.0 %collective-permute-done.47 = bf16[768,1152]{1,0:T(8,128)(2,1)} collective-permute-done((bf16[768,1152]{1,0:T(8,128)(2,1)S(1)}, bf16[768,1152]{1,0:T(8,128)(2,1)}, u32[]{:S(2)}, u32[]{:S(2)}) %collective-permute-start.47) | collective-permute-done | bytes 1769504 | tf_op jit(solution)/shard_map/cond/branch_16_fun/ppermute | solution.py:38
  127.3 3.6 %convert_element_type.112 = f32[768,1152]{1,0:T(8,128)} convert(bf16[768,1152]{1,0:T(8,128)(2,1)} %get-tuple-element.146) | non-fusion elementwise | flops 884736 | bytes 5308416 | tf_op jit(solution)/shard_map/convert_element_type | solution.py:75
  131.0 6.5 %fusion.1 = f32[768,1152]{1,0:T(8,128)} fusion(bf16[768,1152]{1,0:T(8,128)(2,1)} %collective-permute-done.66, bf16[1536,1536]{0,1:T(8,128)(2,1)S(1)} %copy-done.1, f32[]{:T(128)} %bitcast.7, bf16[768,1152]{1,0:T(8,128)(2,1)S(1)} %collective-permute-done.63, bf16[768,1152]{1,0:T(8,128)(2,1)} %get-tuple-element.145), kind=kOutput, calls=%fused_computation.9 | convolution fusion | flops 2727641088 | bytes 11206660 | tf_op jit(solution)/shard_map/dot_general | solution.py:24
  (9 shorter events, 0.0 us)
Async XLA Ops:
  0.6 50.6 %collective-permute-start.62 = (bf16[768,1152]{1,0:T(8,128)(2,1)}, bf16[768,1152]{1,0:T(8,128)(2,1)S(1)}, u32[]{:S(2)}, u32[]{:S(2)}) collective-permute-start(bf16[768,1152]{1,0:T(8,128)(2,1)} %param.68), channel_id=1, source_target_pairs={{0,2},{1,3},{2,0},{3,1},{4,6},{5,7},{6,4},{7,5},{8,10},{9,11},{10,... | collective-permute-start | bytes 5308424 | tf_op jit(solution)/shard_map/ppermute | solution.py:53
  3.4 44.1 %collective-permute-start.16 = (bf16[768,1152]{1,0:T(8,128)(2,1)}, bf16[768,1152]{1,0:T(8,128)(2,1)}, u32[]{:S(2)}, u32[]{:S(2)}) collective-permute-start(bf16[768,1152]{1,0:T(8,128)(2,1)} %param.16), channel_id=1, source_target_pairs={{0,70},{1,71},{2,68},{3,69},{4,66},{5,67},{6,64},{7,65},{8,78},{9,... | collective-permute-start | bytes 5308424 | tf_op jit(solution)/shard_map/cond/branch_16_fun/ppermute | solution.py:38
  47.5 4.1 %collective-permute-start.63 = (bf16[768,1152]{1,0:T(8,128)(2,1)}, bf16[768,1152]{1,0:T(8,128)(2,1)S(1)}, u32[]{:S(2)}, u32[]{:S(2)}) collective-permute-start(bf16[768,1152]{1,0:T(8,128)(2,1)} %get-tuple-element.145), channel_id=1, source_target_pairs={{0,1},{1,0},{2,3},{3,2},{4,5},{5,4},{6,7},{7,6},{8,9},{9,8},{10,11... | collective-permute-start | bytes 5308424 | tf_op jit(solution)/shard_map/ppermute | solution.py:55
  67.0 7.8 %copy-start = (bf16[1536,1536]{0,1:T(8,128)(2,1)}, bf16[1536,1536]{0,1:T(8,128)(2,1)S(1)}, u32[]{:S(2)}) copy-start(bf16[1536,1536]{0,1:T(8,128)(2,1)S(1)} %get-tuple-element.138) | copy-start | bytes 14155780
  73.6 9.1 %collective-permute-start.64 = (f32[768,1152]{1,0:T(8,128)S(1)}, f32[768,1152]{1,0:T(8,128)S(1)}, u32[]{:S(2)}, u32[]{:S(2)}) collective-permute-start(f32[768,1152]{1,0:T(8,128)S(1)} %slice.26), channel_id=1, source_target_pairs={{0,1},{1,0},{2,3},{3,2},{4,5},{5,4},{6,7},{7,6},{8,9},{9,8},{10,11... | collective-permute-start | bytes 10616840 | tf_op jit(solution)/shard_map/ppermute | solution.py:64
  74.2 6.6 %collective-permute-start.65 = (f32[768]{0:T(1024)S(1)}, f32[768]{0:T(1024)S(1)}, u32[]{:S(2)}, u32[]{:S(2)}) collective-permute-start(f32[768]{0:T(1024)S(1)} %slice.28), channel_id=1, source_target_pairs={{0,2},{1,3},{2,0},{3,1},{4,6},{5,7},{6,4},{7,5},{8,10},{9,11},{10,... | collective-permute-start | bytes 9224 | tf_op jit(solution)/shard_map/ppermute | solution.py:68
  80.8 46.6 %collective-permute-start.66 = (bf16[768,1152]{1,0:T(8,128)(2,1)}, bf16[768,1152]{1,0:T(8,128)(2,1)}, u32[]{:S(2)}, u32[]{:S(2)}) collective-permute-start(bf16[768,1152]{1,0:T(8,128)(2,1)} %fusion.3), channel_id=1, source_target_pairs={{0,2},{1,3},{2,0},{3,1},{4,6},{5,7},{6,4},{7,5},{8,10},{9,11},{10,... | collective-permute-start | bytes 5308424 | tf_op jit(solution)/shard_map/ppermute | solution.py:70
  83.3 44.1 %collective-permute-start.47 = (bf16[768,1152]{1,0:T(8,128)(2,1)S(1)}, bf16[768,1152]{1,0:T(8,128)(2,1)}, u32[]{:S(2)}, u32[]{:S(2)}) collective-permute-start(bf16[768,1152]{1,0:T(8,128)(2,1)S(1)} %param.47), channel_id=1, source_target_pairs={{0,70},{1,71},{2,68},{3,69},{4,66},{5,67},{6,64},{7,65},{8,78},{9,... | collective-permute-start | bytes 5308424 | tf_op jit(solution)/shard_map/cond/branch_16_fun/ppermute | solution.py:38
  127.3 3.7 %copy-start.1 = (bf16[1536,1536]{0,1:T(8,128)(2,1)S(1)}, bf16[1536,1536]{0,1:T(8,128)(2,1)}, u32[]{:S(2)}) copy-start(bf16[1536,1536]{0,1:T(8,128)(2,1)} %copy-done) | copy-start | bytes 14155780
where the time goes:
time: 138 us; the launch traced here: 137 us
  waiting for transfers between devices  78 us (57%)
  matrix products  34.2 us (25%)
  starting transfers between devices  14.8 us (11%)
  other arithmetic  4.72 us (3%)
  local copies, waits for them, and re-layouts  2.99 us (2%)
  between operations  2.66 us (2%)
    ppermute x2, waiting for transfers between devices, over_dp(): return lax.ppermute(block, AXES, xor_route(count, partner_mask(rnd, width)))  78 us
    dot_general x4, matrix products, dot(): lax.dot_general(a, b, (dims, ((), ())), preferred_element_type=jnp.float32)  34.2 us
    ppermute x2, starting transfers between devices, over_dp(): return lax.ppermute(block, AXES, xor_route(count, partner_mask(rnd, width)))  10.1 us
    convert_element_type x1, other arithmetic, per_device(): return (image_grad, text_grad.astype(jnp.float32), row_loss)  3.65 us
  transfers between devices with their start and end apart: 7, of which 2 were waited for; matrix products, arithmetic and copies ran while one was open for 7% of the time, Pallas kernels for 0%

commit v1 on v0

--- a/solution.py
+++ b/solution.py
@@ -48,29 +48,40 @@
         text_at = me ^ partner_mask(rnd, width)
         take = lambda device: lax.dynamic_slice_in_dim(ids, device * rows, rows)
         image_ids = jnp.concatenate([take(me), take(me ^ half)])
-        text_ids = jnp.concatenate([take(text_at), take(text_at ^ 1)])
+        own_ids, near_ids = take(text_at), take(text_at ^ 1)
 
         image_far = lax.ppermute(picture, AXES, over_z)
         text_own = by_round(over_dp, rnd - 1, caption)
         text_near = lax.ppermute(text_own, AXES, over_core)
         images = jnp.concatenate([picture, image_far])
-        texts = jnp.concatenate([text_own, text_near])
 
-        logits = scale * dot(images, texts, ((1,), (1,))) + shift
-        pair_loss, coef = pair_terms(logits, image_ids, text_ids)
-        loss_sum = jnp.sum(pair_loss, axis=1)
+        def pairs(text, text_ids):
+            logits = scale * dot(images, text, ((1,), (1,))) + shift
+            pair_loss, coef = pair_terms(logits, image_ids, text_ids)
+            return jnp.sum(pair_loss, axis=1), coef
 
-        text_parts = lax.optimization_barrier(scale * dot(coef, images, ((0,), (0,))))
-        text_far_part = lax.ppermute(text_parts[rows:], AXES, over_core)
-        image_far_part = (scale * dot(coef[rows:], texts, ((1,), (0,)))).astype(jnp.bfloat16)
-        text_part = (text_parts[:rows] + text_far_part).astype(jnp.bfloat16)
+        def image_part(mine):
+            return scale * (
+                dot(own_coef[mine], text_own, ((1,), (0,))) + dot(near_coef[mine], text_near, ((1,), (0,)))
+            )
+
+        own_loss, own_coef = pairs(text_own, own_ids)
+        text_near, own_coef = lax.optimization_barrier((text_near, own_coef))
+        near_loss, near_coef = pairs(text_near, near_ids)
+        loss_sum = own_loss + near_loss
+
+        text_far_part = scale * dot(near_coef, images, ((0,), (0,)))
+        text_far_part = lax.ppermute(text_far_part, AXES, over_core)
+        image_far_part = image_part(slice(rows, None)).astype(jnp.bfloat16)
+        text_part = scale * dot(own_coef, images, ((0,), (0,)))
+        text_part = (text_part + text_far_part).astype(jnp.bfloat16)
 
         loss_far = lax.ppermute(loss_sum[rows:], AXES, over_z)
         image_far_part, loss_far = lax.optimization_barrier((image_far_part, loss_far))
         image_far_part = lax.ppermute(image_far_part, AXES, over_z)
         text_grad = by_round(over_dp, rnd - 1, text_part)
         text_grad, image_far_part = lax.optimization_barrier((text_grad, image_far_part))
-        image_grad = scale * dot(coef[:rows], texts, ((1,), (0,))) + image_far_part.astype(jnp.float32)
+        image_grad = image_part(slice(rows)) + image_far_part.astype(jnp.float32)
         row_loss = (loss_sum[:rows] + loss_far) / (rows * width)
         return image_grad, text_grad.astype(jnp.float32), row_loss
 

time: 138 us -> 151 us (1.094); the launches traced: 137 us -> 148 us
  starting transfers between devices: 14.8 us -> 24.4 us
  matrix products: 34.2 us -> 35.8 us
    ppermute x1, starting transfers between devices: 0.64 us -> 13 us  [per_device(): loss_far = lax.ppermute(loss_sum[rows:], AXES, over_z)]
    ppermute x2, starting transfers between devices: 10.1 us -> 7.05 us  [over_dp(): return lax.ppermute(block, AXES, xor_route(count, partner_mask(rnd, width)))]
    dot_general x4 -> x8, matrix products: 34.2 us -> 35.8 us  [dot(): lax.dot_general(a, b, (dims, ((), ())), preferred_element_type=jnp.float32)]
  transfers between devices with their start and end apart: 7 -> 7, of which waited for: 2 -> 2; matrix products, arithmetic and copies ran while one was open for 7% -> 16% of each run, Pallas kernels for 0% -> 0%
where the time goes in v1:
time: 151 us; the launch traced here: 148 us
  waiting for transfers between devices  78.1 us (52%)
  matrix products  35.8 us (24%)
  starting transfers between devices  24.4 us (16%)
  other arithmetic  4.26 us (3%)
  between operations  2.91 us (2%)
  local copies, waits for them, and re-layouts  2.78 us (2%)
    ppermute x2, waiting for transfers between devices, over_dp(): return lax.ppermute(block, AXES, xor_route(count, partner_mask(rnd, width)))  78 us
    dot_general x8, matrix products, dot(): lax.dot_general(a, b, (dims, ((), ())), preferred_element_type=jnp.float32)  35.8 us
    ppermute x1, starting transfers between devices, per_device(): loss_far = lax.ppermute(loss_sum[rows:], AXES, over_z)  13 us
    ppermute x2, starting transfers between devices, over_dp(): return lax.ppermute(block, AXES, xor_route(count, partner_mask(rnd, width)))  7.05 us
    convert_element_type x1, other arithmetic, per_device(): return (image_grad, text_grad.astype(jnp.float32), row_loss)  3.65 us
  transfers between devices with their start and end apart: 7, of which 2 were waited for; matrix products, arithmetic and copies ran while one was open for 16% of the time, Pallas kernels for 0%

profile of v1, /device:TPU:0, one launch (start us, length us, event | category | flops | bytes accessed | tf_op | source)
XLA Modules:
  0.0 148.2 jit_solution(11714301895904743614)
XLA Ops:
  0.6 2.1 %collective-permute-start.63 = (bf16[768,1152]{1,0:T(8,128)(2,1)}, bf16[768,1152]{1,0:T(8,128)(2,1)S(1)}, u32[]{:S(2)}, u32[]{:S(2)}) collective-permute-start(bf16[768,1152]{1,0:T(8,128)(2,1)} %param.68), channel_id=1, source_target_pairs={{0,2},{1,3},{2,0},{3,1},{4,6},{5,7},{6,4},{7,5},{8,10},{9,11},{10,... | collective-permute-start | bytes 5308424 | tf_op jit(solution)/shard_map/ppermute | solution.py:53
  3.4 42.6 %conditional.2 = (bf16[768,1152]{1,0:T(8,128)(2,1)}) conditional(s32[]{:T(128)} %bitcast.1, bf16[768,1152]{1,0:T(8,128)(2,1)} %param.69, bf16[768,1152]{1,0:T(8,128)(2,1)} %param.69, bf16[768,1152]{1,0:T(8,128)(2,1)} %param.69, bf16[768,1152]{1,0:T(8,128)(2,1)} %param.69, bf16[768,1152]{1,0:T(8,128)(2,1)} %param.69, ...), branch_computations={%region_0.0_spmd, %region_1.0_spmd, %region_2.0_spmd, %region_3.0_... | conditional | bytes 7077936 | solution.py:42
  3.4 3.5 %collective-permute-start.8 = (bf16[768,1152]{1,0:T(8,128)(2,1)}, bf16[768,1152]{1,0:T(8,128)(2,1)}, u32[]{:S(2)}, u32[]{:S(2)}) collective-permute-start(bf16[768,1152]{1,0:T(8,128)(2,1)} %param.8), channel_id=1, source_target_pairs={{0,38},{1,39},{2,36},{3,37},{4,34},{5,35},{6,32},{7,33},{8,46},{9,... | collective-permute-start | bytes 5308424 | tf_op jit(solution)/shard_map/cond/branch_8_fun/ppermute | solution.py:38
  6.9 39.0 %collective-permute-done.8 = bf16[768,1152]{1,0:T(8,128)(2,1)} collective-permute-done((bf16[768,1152]{1,0:T(8,128)(2,1)}, bf16[768,1152]{1,0:T(8,128)(2,1)}, u32[]{:S(2)}, u32[]{:S(2)}) %collective-permute-start.8) | collective-permute-done | bytes 1769504 | tf_op jit(solution)/shard_map/cond/branch_8_fun/ppermute | solution.py:38
  46.0 0.2 collective-permute-start.62
  47.5 0.9 fusion.15
  48.4 1.6 %constant_dynamic-update-slice_fusion.1 = bf16[1536,1152]{1,0:T(8,128)(2,1)S(1)} fusion(bf16[768,1152]{1,0:T(8,128)(2,1)} %param.68), kind=kLoop, calls=%fused_computation.28 | loop fusion | bytes 3538944
  50.0 0.3 constant_dynamic-update-slice_fusion
  50.3 8.2 %add_reduce_fusion.1 = (f32[1536]{0:T(1024)S(1)}, bf16[1536,768]{0,1:T(8,128)(2,1)S(1)}) fusion(s32[768]{0:T(1024)S(1)} %get-tuple-element.148, s32[1536]{0:T(1024)S(1)} %pad_add_fusion, f32[]{:T(128)} %bitcast.22, bf16[1536,1152]{1,0:T(8,128)(2,1)S(1)} %constant_dynamic-update-slice_fusion, bf16[768,1152]{1,0:T(8,128)(2,1)} %get-tuple-element.149, f32[]{:T(128)} %bitcast.17), kind=kOutput, calls=%fused_computation.7 | convolution fusion | flops 2739141120 | bytes 7683080 | tf_op jit(solution)/shard_map/dot_general | solution.py:24
  58.6 6.9 %add_reduce_fusion = (f32[1536]{0:T(1024)S(1)}, bf16[1536,768]{0,1:T(8,128)(2,1)S(1)}) fusion(s32[768]{0:T(1024)S(1)} %get-tuple-element.145, s32[1536]{0:T(1024)S(1)} %pad_add_fusion, f32[]{:T(128)} %bitcast.23, bf16[1536,1152]{1,0:T(8,128)(2,1)S(1)} %constant_dynamic-update-slice_fusion, bf16[768,1152]{1,0:T(8,128)(2,1)S(1)} %collective-permute-done.62, ...), kind=kOutput, calls=%fused_computation.6 | convolution fusion | flops 2739141120 | bytes 7683080 | tf_op jit(solution)/shard_map/dot_general | solution.py:24
  65.5 3.2 %convolution_multiply_fusion = f32[768,1152]{1,0:T(8,128)S(1)} fusion(bf16[1536,768]{0,1:T(8,128)(2,1)S(1)} %get-tuple-element.142, bf16[1536,1152]{1,0:T(8,128)(2,1)S(1)} %constant_dynamic-update-slice_fusion, f32[]{:T(128)} %bitcast.20), kind=kOutput, calls=%fused_computation.10 | convolution fusion | flops 2718793728 | bytes 9437188 | tf_op jit(solution)/shard_map/dot_general | solution.py:24
  68.7 0.6 collective-permute-start.64
  69.3 13.0 %collective-permute-start.65 = (f32[768]{0:T(1024)S(1)}, f32[768]{0:T(1024)S(1)}, u32[]{:S(2)}, u32[]{:S(2)}) collective-permute-start(f32[768]{0:T(1024)S(1)} %slice.26), channel_id=1, source_target_pairs={{0,2},{1,3},{2,0},{3,1},{4,6},{5,7},{6,4},{7,5},{8,10},{9,11},{10,... | collective-permute-start | bytes 9224 | tf_op jit(solution)/shard_map/ppermute | solution.py:79
  82.3 1.7 %fusion.8 = f32[768,1152]{1,0:T(8,128)S(1)} fusion(bf16[768,1152]{1,0:T(8,128)(2,1)S(1)} %collective-permute-done.62, bf16[1536,768]{0,1:T(8,128)(2,1)S(1)} %get-tuple-element.142), kind=kOutput, calls=%fused_computation.20 | convolution fusion | flops 1358954496 | bytes 6488064 | tf_op jit(solution)/shard_map/dot_general | solution.py:24
  84.0 3.3 %fusion.7 = bf16[768,1152]{1,0:T(8,128)(2,1)S(1)} fusion(f32[768,1152]{1,0:T(8,128)S(1)} %fusion.8, bf16[768,1152]{1,0:T(8,128)(2,1)} %get-tuple-element.149, f32[]{:T(128)} %bitcast.19, bf16[1536,768]{0,1:T(8,128)(2,1)S(1)} %get-tuple-element.135), kind=kOutput, calls=%fused_computation.19 | convolution fusion | flops 1361608704 | bytes 8257540 | tf_op jit(solution)/shard_map/dot_general | solution.py:24
  87.4 1.5 %collective-permute-start.66 = (bf16[768,1152]{1,0:T(8,128)(2,1)S(1)}, bf16[768,1152]{1,0:T(8,128)(2,1)S(1)}, u32[]{:S(2)}, u32[]{:S(2)}) collective-permute-start(bf16[768,1152]{1,0:T(8,128)(2,1)S(1)} %fusion.7), channel_id=1, source_target_pairs={{0,2},{1,3},{2,0},{3,1},{4,6},{5,7},{6,4},{7,5},{8,10},{9,11},{10,... | collective-permute-start | bytes 5308424 | tf_op jit(solution)/shard_map/ppermute | solution.py:81
  88.9 3.5 %fusion.10 = f32[768,1152]{1,0:T(8,128)} fusion(bf16[768,1152]{1,0:T(8,128)(2,1)S(1)} %copy-done.1, bf16[1536,768]{0,1:T(8,128)(2,1)S(1)} %get-tuple-element.142), kind=kOutput, calls=%fused_computation.22 | convolution fusion | flops 1358954496 | bytes 6488064 | tf_op jit(solution)/shard_map/dot_general | solution.py:24
  92.4 0.6 fusion.14
  93.0 3.2 %fusion.6 = bf16[768,1152]{1,0:T(8,128)(2,1)S(1)} fusion(f32[768,1152]{1,0:T(8,128)S(1)} %collective-permute-done.64, bf16[1536,768]{0,1:T(8,128)(2,1)S(1)} %get-tuple-element.135, bf16[1536,1152]{1,0:T(8,128)(2,1)S(1)} %constant_dynamic-update-slice_fusion, f32[]{:T(128)} %bitcast.21), kind=kOutput, calls=%fused_computation.18 | convolution fusion | flops 2720563200 | bytes 11206660 | tf_op jit(solution)/shard_map/dot_general | solution.py:24
  96.2 42.6 %conditional.3 = (bf16[768,1152]{1,0:T(8,128)(2,1)}) conditional(s32[]{:T(128)} %bitcast.1, bf16[768,1152]{1,0:T(8,128)(2,1)S(1)} %fusion.6, bf16[768,1152]{1,0:T(8,128)(2,1)S(1)} %fusion.6, bf16[768,1152]{1,0:T(8,128)(2,1)S(1)} %fusion.6, bf16[768,1152]{1,0:T(8,128)(2,1)S(1)} %fusion.6, ...), branch_computations={%region_31.32_spmd, %region_32.33_spmd, %region_33.34_spmd, %regio... | conditional | bytes 7077936 | solution.py:42
  96.2 3.5 %collective-permute-start.39 = (bf16[768,1152]{1,0:T(8,128)(2,1)S(1)}, bf16[768,1152]{1,0:T(8,128)(2,1)}, u32[]{:S(2)}, u32[]{:S(2)}) collective-permute-start(bf16[768,1152]{1,0:T(8,128)(2,1)S(1)} %param.39), channel_id=1, source_target_pairs={{0,38},{1,39},{2,36},{3,37},{4,34},{5,35},{6,32},{7,33},{8,46},{9,... | collective-permute-start | bytes 5308424 | tf_op jit(solution)/shard_map/cond/branch_8_fun/ppermute | solution.py:38
  99.7 39.0 %collective-permute-done.39 = bf16[768,1152]{1,0:T(8,128)(2,1)} collective-permute-done((bf16[768,1152]{1,0:T(8,128)(2,1)S(1)}, bf16[768,1152]{1,0:T(8,128)(2,1)}, u32[]{:S(2)}, u32[]{:S(2)}) %collective-permute-start.39) | collective-permute-done | bytes 1769504 | tf_op jit(solution)/shard_map/cond/branch_8_fun/ppermute | solution.py:38
  138.8 3.6 %convert_element_type.116 = f32[768,1152]{1,0:T(8,128)} convert(bf16[768,1152]{1,0:T(8,128)(2,1)} %get-tuple-element.150) | non-fusion elementwise | flops 884736 | bytes 5308416 | tf_op jit(solution)/shard_map/convert_element_type | solution.py:86
  142.4 5.6 %fusion.5 = f32[768,1152]{1,0:T(8,128)} fusion(f32[768,1152]{1,0:T(8,128)S(1)} %copy-done.2, bf16[768,1152]{1,0:T(8,128)(2,1)} %get-tuple-element.149, bf16[768,1152]{1,0:T(8,128)(2,1)S(1)} %collective-permute-done.66, f32[]{:T(128)} %bitcast.16, bf16[1536,768]{0,1:T(8,128)(2,1)} %copy-done.3), kind=kOutput, calls=%fused_computation.17 | convolution fusion | flops 1362493440 | bytes 11796992 | tf_op jit(solution)/shard_map/dot_general | solution.py:24
  (16 shorter events, 0.1 us)
Async XLA Ops:
  0.6 49.4 %collective-permute-start.63 = (bf16[768,1152]{1,0:T(8,128)(2,1)}, bf16[768,1152]{1,0:T(8,128)(2,1)S(1)}, u32[]{:S(2)}, u32[]{:S(2)}) collective-permute-start(bf16[768,1152]{1,0:T(8,128)(2,1)} %param.68), channel_id=1, source_target_pairs={{0,2},{1,3},{2,0},{3,1},{4,6},{5,7},{6,4},{7,5},{8,10},{9,11},{10,... | collective-permute-start | bytes 5308424 | tf_op jit(solution)/shard_map/ppermute | solution.py:53
  3.4 42.6 %collective-permute-start.8 = (bf16[768,1152]{1,0:T(8,128)(2,1)}, bf16[768,1152]{1,0:T(8,128)(2,1)}, u32[]{:S(2)}, u32[]{:S(2)}) collective-permute-start(bf16[768,1152]{1,0:T(8,128)(2,1)} %param.8), channel_id=1, source_target_pairs={{0,38},{1,39},{2,36},{3,37},{4,34},{5,35},{6,32},{7,33},{8,46},{9,... | collective-permute-start | bytes 5308424 | tf_op jit(solution)/shard_map/cond/branch_8_fun/ppermute | solution.py:38
  46.0 12.6 %collective-permute-start.62 = (bf16[768,1152]{1,0:T(8,128)(2,1)}, bf16[768,1152]{1,0:T(8,128)(2,1)S(1)}, u32[]{:S(2)}, u32[]{:S(2)}) collective-permute-start(bf16[768,1152]{1,0:T(8,128)(2,1)} %get-tuple-element.149), channel_id=1, source_target_pairs={{0,1},{1,0},{2,3},{3,2},{4,5},{5,4},{6,7},{7,6},{8,9},{9,8},{10,11... | collective-permute-start | bytes 5308424 | tf_op jit(solution)/shard_map/ppermute | solution.py:55
  58.5 34.5 %copy-start.3 = (bf16[1536,768]{0,1:T(8,128)(2,1)}, bf16[1536,768]{0,1:T(8,128)(2,1)S(1)}, u32[]{:S(2)}) copy-start(bf16[1536,768]{0,1:T(8,128)(2,1)S(1)} %get-tuple-element.135) | copy-start | bytes 7077892
  58.5 23.7 %copy-start = (bf16[768,1152]{1,0:T(8,128)(2,1)}, bf16[768,1152]{1,0:T(8,128)(2,1)S(1)}, u32[]{:S(2)}) copy-start(bf16[768,1152]{1,0:T(8,128)(2,1)S(1)} %collective-permute-done.62) | copy-start | bytes 5308420
  68.7 24.3 %collective-permute-start.64 = (f32[768,1152]{1,0:T(8,128)S(1)}, f32[768,1152]{1,0:T(8,128)S(1)}, u32[]{:S(2)}, u32[]{:S(2)}) collective-permute-start(f32[768,1152]{1,0:T(8,128)S(1)} %convolution_multiply_fusion), channel_id=1, source_target_pairs={{0,1},{1,0},{2,3},{3,2},{4,5},{5,4},{6,7},{7,6},{8,9},{9,8},{10,11... | collective-permute-start | bytes 10616840 | tf_op jit(solution)/shard_map/ppermute | solution.py:74
  69.3 18.1 %collective-permute-start.65 = (f32[768]{0:T(1024)S(1)}, f32[768]{0:T(1024)S(1)}, u32[]{:S(2)}, u32[]{:S(2)}) collective-permute-start(f32[768]{0:T(1024)S(1)} %slice.26), channel_id=1, source_target_pairs={{0,2},{1,3},{2,0},{3,1},{4,6},{5,7},{6,4},{7,5},{8,10},{9,11},{10,... | collective-permute-start | bytes 9224 | tf_op jit(solution)/shard_map/ppermute | solution.py:79
  84.0 4.9 %copy-start.1 = (bf16[768,1152]{1,0:T(8,128)(2,1)S(1)}, bf16[768,1152]{1,0:T(8,128)(2,1)}, u32[]{:S(2)}) copy-start(bf16[768,1152]{1,0:T(8,128)(2,1)} %copy-done) | copy-start | bytes 5308420
  87.4 51.4 %collective-permute-start.66 = (bf16[768,1152]{1,0:T(8,128)(2,1)S(1)}, bf16[768,1152]{1,0:T(8,128)(2,1)S(1)}, u32[]{:S(2)}, u32[]{:S(2)}) collective-permute-start(bf16[768,1152]{1,0:T(8,128)(2,1)S(1)} %fusion.7), channel_id=1, source_target_pairs={{0,2},{1,3},{2,0},{3,1},{4,6},{5,7},{6,4},{7,5},{8,10},{9,11},{10,... | collective-permute-start | bytes 5308424 | tf_op jit(solution)/shard_map/ppermute | solution.py:81
  96.2 42.5 %collective-permute-start.39 = (bf16[768,1152]{1,0:T(8,128)(2,1)S(1)}, bf16[768,1152]{1,0:T(8,128)(2,1)}, u32[]{:S(2)}, u32[]{:S(2)}) collective-permute-start(bf16[768,1152]{1,0:T(8,128)(2,1)S(1)} %param.39), channel_id=1, source_target_pairs={{0,38},{1,39},{2,36},{3,37},{4,34},{5,35},{6,32},{7,33},{8,46},{9,... | collective-permute-start | bytes 5308424 | tf_op jit(solution)/shard_map/cond/branch_8_fun/ppermute | solution.py:38
  138.8 3.7 %copy-start.2 = (f32[768,1152]{1,0:T(8,128)S(1)}, f32[768,1152]{1,0:T(8,128)}, u32[]{:S(2)}) copy-start(f32[768,1152]{1,0:T(8,128)} %fusion.10) | copy-start | bytes 10616836
